TPU v7x, 512 devices: a whole 4x4x16 slice. The times are simulated.
512 devices in a mesh: grp: 8 (over y, core), dev: 64 (over x, z).
Axes of the slice: x: 4, y: 4, z: 16, core: 2. Of those that a mesh axis runs over, the one named last changes fastest.
Arguments:
- embeddings: bfloat16 [196608, 4096], P(('grp', 'dev')), may hold values from -256 to 256
- sketch_matrix: bfloat16 [4096, 128], P('dev'), may hold values from -0.09375 to 0.09375
Outputs:
- orthobasis: float32 [196608, 128], P(('grp', 'dev'))
- projected: float32 [4096, 128], P('dev')
All inputs are finite; a program needn't handle non-finite values.
Results may differ from a plain program's by a relative error of at most 0.0065.
Values may be sent and summed in bfloat16 or wider, within the bound.
A program may use at most 64 MiB of HBM per device.

v0:
```python
import jax
import jax.numpy as jnp
from jax import lax
from jax.sharding import PartitionSpec as P


def swapped(x, axis, apart):
    return lax.ppermute(x, axis, [(i, i ^ 1 << apart) for i in range(lax.axis_size(axis))])


def contract_rows(left, right):
    return lax.dot_general(
        left, right, (((0,), (0,)), ((), ())), preferred_element_type=jnp.float32
    )


def merge_factor(triangle, partner):
    summed = jnp.dot(triangle, triangle.T, precision=lax.Precision.HIGHEST) + jnp.dot(
        partner, partner.T, precision=lax.Precision.HIGHEST
    )
    return jnp.linalg.cholesky(summed)


def body(embeddings, sketch_matrix):
    groups = lax.axis_size("grp")
    members = lax.axis_size("dev")
    local_rows = embeddings.shape[0]
    width_all = embeddings.shape[1]
    row_total = local_rows * groups * members
    columns = embeddings
    sketched = jnp.dot(
        columns,
        lax.all_gather(sketch_matrix, "dev", axis=0, tiled=True),
        preferred_element_type=jnp.float32,
    ).astype(jnp.bfloat16)
    summed = lax.psum(contract_rows(embeddings, sketched), ("grp", "dev"))
    powered = (summed / row_total).astype(jnp.bfloat16)
    refined = jnp.dot(embeddings, powered, preferred_element_type=jnp.float32)
    gram_local = jnp.dot(refined.T, refined, precision=lax.Precision.HIGHEST) / row_total
    triangle = jnp.linalg.cholesky(gram_local)
    for section_bit in range(members.bit_length() - 1):
        partner = swapped(triangle.astype(jnp.bfloat16), "dev", section_bit).astype(triangle.dtype)
        triangle = merge_factor(triangle, partner)
    for section_bit in range(groups.bit_length() - 1):
        partner = swapped(triangle.astype(jnp.bfloat16), "grp", section_bit).astype(triangle.dtype)
        triangle = merge_factor(triangle, partner)
    orthobasis = jax.scipy.linalg.solve_triangular(triangle, refined.T, lower=True).T
    basis_half = orthobasis.astype(jnp.bfloat16)
    out_scale = width_all**0.5 / row_total
    columns = embeddings
    partial_rows = lax.psum_scatter(
        contract_rows(columns, basis_half), "dev", scatter_dimension=0, tiled=True
    )
    projected = lax.psum(partial_rows, "grp") * out_scale
    return (orthobasis, projected)


def solution(mesh):
    in_specs = (P(("grp", "dev"), None), P("dev", None))
    out_specs = (P(("grp", "dev"), None), P("dev", None))
    return jax.shard_map(body, mesh=mesh, in_specs=in_specs, out_specs=out_specs, check_vma=False)
```

profile of v0, /device:TPU:1, one launch (start us, length us, event | category | flops | bytes accessed | tf_op | source)
XLA Modules:
  0.0 1573.3 jit_solution(13973858230422439947)
XLA Ops:
  8.0 137.8 %all-gather.2.cloned.1.call-done = bf16[4096,128]{1,0:T(8,128)(2,1)} async-done(((bf16[64,128]{1,0:T(8,128)(2,1)}), bf16[4096,128]{1,0:T(8,128)(2,1)}) %all-gather.2.cloned.1.call-update) | async-done | bytes 1048592 | tf_op jit(solution)/shard_map/all_gather | solution.py:33
  145.7 5.3 convolution_bitcast_fusion.1
  151.1 481.4 %all-reduce.2.cloned.1.call-done = f32[4096,128]{0,1:T(8,128)} async-done(((f32[4096,128]{0,1:T(8,128)}), f32[4096,128]{0,1:T(8,128)}) %all-reduce.2.cloned.1.call-update) | async-done | bytes 2097168 | tf_op jit(solution)/shard_map/psum | solution.py:36
  635.6 11.7 cholesky.164
  653.6 11.7 cholesky.175
  666.7 4.3 collective-permute-start.1
  672.5 11.7 cholesky.186
  685.6 6.6 collective-permute-start.2
  694.4 11.7 cholesky.197
  707.5 9.4 collective-permute-start.3
  721.1 11.7 cholesky.208
  734.2 3.8 collective-permute-start.4
  739.5 11.7 cholesky.219
  752.6 4.3 collective-permute-start.5
  759.0 11.7 cholesky.230
  772.1 10.0 collective-permute-start.6
  783.3 11.7 cholesky.241
  796.3 3.2 collective-permute-start.7
  801.3 11.7 cholesky.252
  814.3 3.5 collective-permute-start.8
  820.8 11.7 cholesky.263
  833.8 10.4 custom-call.6
  850.6 681.5 %reduce-scatter.4.cloned.1.call-done = f32[64,128]{1,0:T(8,128)} async-done(((f32[4096,128]{1,0:T(8,128)}), f32[64,128]{1,0:T(8,128)}) %reduce-scatter.4.cloned.1.call-update) | async-done | bytes 32784
  1533.0 32.6 %psum.15 = f32[64,128]{0,1:T(8,128)S(1)} all-reduce(f32[64,128]{0,1:T(8,128)S(1)} %copy.84), channel_id=1, replica_groups=mesh['grp'=8,'dev'=64] {'grp'}, use_global_device_ids=true, to_apply=%region_4.6 | all-reduce | flops 8192 | bytes 65536 | tf_op jit(solution)/shard_map/psum | solution.py:54
  (96 shorter events, 47.5 us)
Async XLA Ops:
  7.2 138.6 %copy-start = (bf16[384,4096]{1,0:T(8,128)(2,1)S(1)}, bf16[384,4096]{1,0:T(8,128)(2,1)}, u32[]{:S(2)}) copy-start(bf16[384,4096]{1,0:T(8,128)(2,1)} %param.3) | copy-start | bytes 9437188
  7.2 138.5 %all-gather.2.cloned.1.call-start = ((), (), s32[]{:S(2)}) async-start(), calls=%async_computation.1 | async-start | bytes 1064960 | tf_op jit(solution)/shard_map/all_gather | solution.py:33
  7.9 624.6 %all-reduce.2.cloned.1.call-start = ((), (), s32[]{:S(2)}) async-start(), calls=%async_computation.2 | async-start | bytes 4194304 | tf_op jit(solution)/shard_map/psum | solution.py:36
  151.0 1381.1 %reduce-scatter.4.cloned.1.call-start = ((), (), s32[]{:S(2)}) async-start(), calls=%async_computation.3 | async-start | bytes 2129920
  648.7 4.7 collective-permute-start
  666.7 5.6 collective-permute-start.1
  685.6 8.6 collective-permute-start.2
  707.5 13.4 collective-permute-start.3
  734.2 5.1 collective-permute-start.4
  752.6 6.2 collective-permute-start.5
  772.1 10.9 collective-permute-start.6
  796.3 4.7 collective-permute-start.7
  814.3 6.2 collective-permute-start.8
  845.6 5.0 copy-start.1
Sparse Core Ops, SparseCore 0:
  11.0 134.7 all-gather.1
  151.2 481.2 all-reduce.1
  850.7 681.3 reduce-scatter.3
where the time goes:
time: 1580 us; the launch traced here: 1570 us
  waiting for transfers between devices  1310 us (83%)
  other arithmetic  141 us (9%)
  starting transfers between devices  47.1 us (3%)
  blocking collectives  32.6 us (2%)
  matrix products  21.1 us (1%)
    unnamed x4, waiting for transfers between devices  682 us
    psum x1, waiting for transfers between devices, body(): summed = lax.psum(contract_rows(embeddings, sketched), ('grp', 'dev'))  481 us
    all_gather x1, waiting for transfers between devices, body(): lax.all_gather(sketch_matrix, 'dev', axis=0, tiled=True)  138 us
    another operation x27, other arithmetic, merge_factor(): return jnp.linalg.cholesky(summed)  111 us
    ppermute x9, starting transfers between devices, swapped(): lax.ppermute(x, axis, [(i, i ^ 1 << apart) for i in range(lax.axis_size(a...  47 us
    psum x1, blocking collectives, body(): projected = lax.psum(partial_rows, 'grp') * out_scale  32.6 us
  transfers between devices with their start and end apart: 12, of which 11 were waited for; matrix products, arithmetic and copies ran while one was open for 1% of the time, Pallas kernels for 0%

commit v1 on v0

v1 whole, which is shorter than its diff:
```python
import jax
import jax.numpy as jnp
from jax import lax
from jax.experimental import pallas as pl
from jax.experimental.pallas import tpu as pltpu
from jax.sharding import PartitionSpec as P

X, Y, Z, C = 4, 4, 16, 2
XY = X * Y
ZL = Z // C
DEVICES = XY * Z * C
PIECE = 16
CHUNK = ZL * Y * PIECE
PANEL = 16
HIGHEST = lax.Precision.HIGHEST
F32, BF16 = jnp.float32, jnp.bfloat16


def nt(a, b, precision=None):
    return lax.dot_general(
        a, b, (((1,), (1,)), ((), ())), precision=precision, preferred_element_type=F32
    )


def tn(a, b, precision=None):
    return lax.dot_general(
        a, b, (((0,), (0,)), ((), ())), precision=precision, preferred_element_type=F32
    )


def nn(a, b, precision=None):
    return jnp.dot(a, b, precision=precision, preferred_element_type=F32)


def inverse_factor_steps(gram):
    k = gram.shape[0]
    rows = lax.broadcasted_iota(jnp.int32, (PANEL, 1), 0)
    eye = (
        lax.broadcasted_iota(jnp.int32, (k, k), 0) == lax.broadcasted_iota(jnp.int32, (k, k), 1)
    ).astype(F32)
    trailing = jnp.concatenate([gram, eye], axis=1)
    done = []
    for base in range(0, k, PANEL):
        panel = trailing[:PANEL]
        cols = [
            jnp.broadcast_to(panel[:, base + t : base + t + 1], (PANEL, k)) for t in range(PANEL)
        ]
        left, right = panel[:, :k], panel[:, k:]
        for j in range(PANEL):
            pivot = lax.rsqrt(cols[j][j : j + 1])
            factor = cols[j] * pivot
            below = jnp.where(rows > j, factor, 0.0)
            for t in range(j + 1, PANEL):
                cols[t] = cols[t] - below * factor[t : t + 1]
            scale = jnp.where(rows == j, pivot, 1.0)
            left_row, right_row = left[j : j + 1] * pivot, right[j : j + 1] * pivot
            left = left * scale - below * left_row
            right = right * scale - below * right_row
        done.append(right)
        if base + PANEL < k:
            both = jnp.concatenate([left, right], axis=1)
            trailing = trailing[PANEL:] - tn(left[:, base + PANEL :], both, HIGHEST)
            yield None
    yield jnp.concatenate(done, axis=0)


def kernel(
    e_hbm, s_ref, ortho_ref, proj_ref,
    e_ref, s_full, p_full, part_a, part_b, core_a, core_b, sum_a, sum_b, xy_a, xy_b,
    zout_a, zout_b, z_a, z_b, gpart, g1, g2, gfull, yfin,
    load_sem,
    ags_z_s, ags_z_r, ags_x_s, ags_x_r, ags_c_s, ags_c_r,
    agp_z_s, agp_z_r, agp_x_s, agp_x_r, agp_c_s, agp_c_r,
    rsa_c_s, rsa_c_r, rsa_x_s, rsa_x_r, rsa_z_s, rsa_z_r,
    rsb_c_s, rsb_c_r, rsb_x_s, rsb_x_r, rsb_z_s, rsb_z_r,
    g1_s, g1_r, g2_s, g2_r, g3_s, g3_r, f_s, f_r,
):
    grp, dev = lax.axis_index("grp"), lax.axis_index("dev")
    y, c = grp // C, grp % C
    x, z = dev // Z, dev % Z
    other = 1 - c
    half, zl = z // ZL, z % ZL
    owner = c == half
    rows_all = DEVICES * e_ref.shape[0]

    def at(x_, y_, z_, c_):
        return (y_ * C + c_, x_ * Z + z_)

    def xy(k):
        kx, ky = k // Y, k % Y
        return ((x + kx) % X, (y + ky) % Y), ((x + X - kx) % X, (y + Y - ky) % Y)

    drains = []

    def send(src, dst, ssem, rsem, to, when=None):
        copy = pltpu.make_async_remote_copy(
            src_ref=src, dst_ref=dst, send_sem=ssem, recv_sem=rsem,
            device_id=to, device_id_type=pl.DeviceIdType.MESH,
        )

        def start():
            copy.start()

        def drain():
            copy.wait_send()

        if when is None:
            start()
            drains.append(drain)
        else:
            pl.when(when)(start)
            drains.append(lambda: pl.when(when)(drain))

    def receive(dst, ssem, rsem, when=None):
        copy = pltpu.make_async_remote_copy(
            src_ref=dst, dst_ref=dst, send_sem=ssem, recv_sem=rsem,
            device_id=at(x, y, z, other), device_id_type=pl.DeviceIdType.MESH,
        )
        if when is None:
            copy.wait_recv()
        else:
            pl.when(when)(copy.wait_recv)

    load = pltpu.make_async_copy(e_hbm, e_ref, load_sem)
    load.start()

    barrier = pltpu.get_barrier_semaphore()

    def greet_plane(i, _):
        (x_, y_), _b = xy(i // C)
        pl.semaphore_signal(
            barrier, inc=1, device_id=at(x_, y_, z, (c + i % C) % C),
            device_id_type=pl.DeviceIdType.MESH,
        )
        return 0

    def greet_line(i, _):
        pl.semaphore_signal(
            barrier, inc=1, device_id=at(x, y, (z + i // C) % Z, (c + i % C) % C),
            device_id_type=pl.DeviceIdType.MESH,
        )
        return 0

    lax.fori_loop(1, XY * C, greet_plane, 0)
    lax.fori_loop(C, Z * C, greet_line, 0)
    pl.semaphore_wait(barrier, XY * C - 1 + Z * C - C)

    def gather(piece, full, z_s, z_r, x_s, x_r, c_s, c_r):
        @pl.when(owner)
        def _():
            full[x, c, zl, y] = piece()

        for k in range(1, Z):
            mine = full.at[x, c, zl, y]
            send(mine, mine, z_s.at[k], z_r.at[zl], at(x, y, (z + k) % Z, c), owner)
        for k in range(ZL):
            low = (zl + k) % ZL
            receive(
                full.at[x, c, low, y], z_s.at[0], z_r.at[low],
                jnp.logical_not(owner) if k == 0 else None,
            )
        mine = full.at[x, c, :, y]
        for k in range(1, XY):
            (x_, y_), _b = xy(k)
            send(mine, mine, x_s.at[k], x_r.at[k], at(x_, y_, z, c))
        send(mine, mine, c_s.at[0], c_r.at[0], at(x, y, z, other))
        for k in range(1, XY):
            _f, (x_, y_) = xy(k)
            got = full.at[x_, c, :, y_]
            receive(got, x_s.at[k], x_r.at[k])
            send(got, got, c_s.at[k], c_r.at[k], at(x, y, z, other))
        for k in range(XY):
            _f, (x_, y_) = xy(k)
            receive(full.at[x_, other, :, y_], c_s.at[k], c_r.at[k])

    def times_full(full):
        def step(i, total):
            columns = pl.ds(pl.multiple_of(i * CHUNK, CHUNK), CHUNK)
            block = full[i // C, i % C].reshape(CHUNK, full.shape[-1])
            return total + nn(e_ref[:, columns], block)

        return lax.fori_loop(
            0, X * C, step, jnp.zeros((e_ref.shape[0], full.shape[-1]), F32)
        )

    def scatter_first(left, part, core, summed, landing, c_s, c_r, x_s, x_r):
        def product(kx, half_, slot):
            start = pl.multiple_of(((x + kx) % X) * (C * CHUNK) + half_ * CHUNK, CHUNK)
            block = nn(left, e_ref[:, pl.ds(start, CHUNK)])
            k = left.shape[0]
            block = jnp.concatenate(
                [block[:, i : i + k].T for i in range(0, CHUNK, k)], axis=0
            ).astype(BF16)
            block = block.reshape(ZL, Y, PIECE, k)
            for y_ in range(Y):
                part[kx, slot, y_] = block[:, y_]

        order = (1, 2, 3, 0)
        for kx in order:
            product(kx, other, 0)
            send(part.at[kx, 0], core.at[kx], c_s.at[kx], c_r.at[kx], at(x, y, z, other))
            product(kx, c, 1)
        for kx in order:
            receive(core.at[kx], c_s.at[kx], c_r.at[kx])
            summed[kx] = (part[kx, 1].astype(F32) + core[kx].astype(F32)).astype(BF16)
            for ky in (1, 2, 3, 0):
                k = kx * Y + ky
                if k:
                    (x_, y_), _b = xy(k)
                    send(
                        summed.at[kx, y_], landing.at[k], x_s.at[k], x_r.at[k], at(x_, y_, z, c)
                    )

    def scatter_second(summed, landing, x_s, x_r, zout, zland, z_s, z_r):
        total = summed[0, y].astype(F32)
        for k in range(1, XY):
            receive(landing.at[k], x_s.at[k], x_r.at[k])
            total = total + landing[k].astype(F32)
        zout[...] = total.astype(BF16)
        for k in range(ZL):
            low = (zl + k) % ZL
            send(
                zout.at[low], zland.at[z], z_s.at[k], z_r.at[z], at(x, y, c * ZL + low, c),
                jnp.logical_not(owner) if k == 0 else None,
            )

    def scatter_third(zout, zland, z_s, z_r):
        zland[z] = zout[zl]
        total = None
        for k in range(1, Z):
            from_ = (z + k) % Z
            receive(zland.at[from_], z_s.at[0], z_r.at[from_])
        for k in range(Z):
            term = zland[k].astype(F32)
            total = term if total is None else total + term
        return total

    gather(
        lambda: s_ref[pl.ds(pl.multiple_of(y * PIECE, PIECE), PIECE), :],
        s_full, ags_z_s, ags_z_r, ags_x_s, ags_x_r, ags_c_s, ags_c_r,
    )
    load.wait()
    sketched = times_full(s_full).T.astype(BF16)

    scatter_first(sketched, part_a, core_a, sum_a, xy_a, rsa_c_s, rsa_c_r, rsa_x_s, rsa_x_r)
    scatter_second(sum_a, xy_a, rsa_x_s, rsa_x_r, zout_a, z_a, rsa_z_s, rsa_z_r)
    gather(
        lambda: (scatter_third(zout_a, z_a, rsa_z_s, rsa_z_r) / rows_all).astype(BF16),
        p_full, agp_z_s, agp_z_r, agp_x_s, agp_x_r, agp_c_s, agp_c_r,
    )

    refined = times_full(p_full)
    refined_t = refined.T
    gram = nn(refined_t, refined, HIGHEST) / rows_all
    gpart[...] = gram.reshape(gpart.shape)

    for k in range(XY):
        (x_, y_), _b = xy(k)
        when = jnp.logical_not(owner) if k == 0 else None
        send(
            gpart.at[x_ * Y + y_], g1.at[C * k + c], g1_s.at[k], g1_r.at[C * k + c],
            at(x_, y_, z, half), when,
        )

    scatter_first(
        refined_t.astype(BF16), part_b, core_b, sum_b, xy_b, rsb_c_s, rsb_c_r, rsb_x_s, rsb_x_r
    )

    @pl.when(owner)
    def _():
        g1[c] = gpart[x * Y + y]
        for k in range(1, XY):
            for c_ in range(C):
                receive(g1.at[C * k + c_], g1_s.at[0], g1_r.at[C * k + c_])
        receive(g1.at[other], g1_s.at[0], g1_r.at[other])
        g2[z] = jnp.sum(g1[...], axis=0)

    for k in range(1, Z):
        z_ = (z + k) % Z
        send(g2.at[z], g2.at[z], g2_s.at[k], g2_r.at[z], at(x, y, z_, z_ // ZL), owner)

    @pl.when(owner)
    def _():
        for k in range(1, Z):
            from_ = (z + k) % Z
            receive(g2.at[from_], g2_s.at[0], g2_r.at[from_])
        gfull[x * Y + y] = jnp.sum(g2[...], axis=0)

    for i in range(1, XY * C):
        (x_, y_), _b = xy(i // C)
        mine = gfull.at[x * Y + y]
        send(
            mine, mine, g3_s.at[i], g3_r.at[i // C], at(x_, y_, z, (c + i % C) % C), owner
        )

    scatter_second(sum_b, xy_b, rsb_x_s, rsb_x_r, zout_b, z_b, rsb_z_s, rsb_z_r)
    for k in range(XY):
        _f, (x_, y_) = xy(k)
        receive(
            gfull.at[x_ * Y + y_], g3_s.at[0], g3_r.at[k],
            jnp.logical_not(owner) if k == 0 else None,
        )

    steps = inverse_factor_steps(gfull[...].reshape(gram.shape))
    for i, inverse in enumerate(steps):
        if i == 4:

            @pl.when(owner)
            def _():
                yfin[y] = scatter_third(zout_b, z_b, rsb_z_s, rsb_z_r)

            for j in range(1, Y * C):
                y_, c_ = (y + j // C) % Y, (c + j % C) % C
                send(yfin.at[y], yfin.at[y], f_s.at[j], f_r.at[y], at(x, y_, z, c_), owner)

    ortho_ref[...] = nt(refined, inverse, HIGHEST)
    for k in range(Y):
        from_ = (y + k) % Y
        receive(
            yfin.at[from_], f_s.at[0], f_r.at[from_], jnp.logical_not(owner) if k == 0 else None
        )
    scale = e_ref.shape[1] ** 0.5 / rows_all
    proj_ref[...] = nt(yfin[...].reshape(proj_ref.shape), inverse, HIGHEST) * scale

    for drain in drains:
        drain()


def body(embeddings, sketch_matrix):
    rows, width = embeddings.shape
    k = sketch_matrix.shape[1]
    dma = pltpu.SemaphoreType.DMA
    full = pltpu.VMEM((X, C, ZL, Y, PIECE, k), BF16)
    part = pltpu.VMEM((X, C, Y, ZL, PIECE, k), BF16)
    core = pltpu.VMEM((X, Y, ZL, PIECE, k), BF16)
    landing = pltpu.VMEM((XY, ZL, PIECE, k), BF16)
    zout = pltpu.VMEM((ZL, PIECE, k), BF16)
    zland = pltpu.VMEM((Z, PIECE, k), BF16)
    gather_sems = [dma((Z,)), dma((ZL,)), dma((XY,)), dma((XY,)), dma((XY,)), dma((XY,))]
    scatter_sems = [dma((X,)), dma((X,)), dma((XY,)), dma((XY,)), dma((ZL,)), dma((Z,))]
    return pl.pallas_call(
        kernel,
        out_shape=(
            jax.ShapeDtypeStruct((rows, k), F32),
            jax.ShapeDtypeStruct(sketch_matrix.shape, F32),
        ),
        in_specs=[pl.BlockSpec(memory_space=pl.ANY), pl.BlockSpec(memory_space=pltpu.VMEM)],
        out_specs=[pl.BlockSpec(memory_space=pltpu.VMEM)] * 2,
        scratch_shapes=[
            pltpu.VMEM((rows, width), BF16),
            full, full, part, part, core, core, core, core, landing, landing,
            zout, zout, zland, zland,
            pltpu.VMEM((XY, k // XY, k), F32),
            pltpu.VMEM((XY * C, k // XY, k), F32),
            pltpu.VMEM((Z, k // XY, k), F32),
            pltpu.VMEM((XY, k // XY, k), F32),
            pltpu.VMEM((Y, PIECE, k), F32),
            dma,
            *gather_sems, *gather_sems, *scatter_sems, *scatter_sems,
            dma((XY,)), dma((XY * C,)), dma((Z,)), dma((Z,)), dma((XY * C,)), dma((XY,)),
            dma((Y * C,)), dma((Y,)),
        ],
        compiler_params=pltpu.CompilerParams(
            collective_id=0, has_side_effects=True, vmem_limit_bytes=40 * 1024 * 1024
        ),
        cost_estimate=pl.CostEstimate(
            flops=8 * rows * width * k, bytes_accessed=2 * rows * width, transcendentals=0
        ),
    )(embeddings, sketch_matrix)


def solution(mesh):
    in_specs = (P(("grp", "dev"), None), P("dev", None))
    out_specs = (P(("grp", "dev"), None), P("dev", None))
    return jax.shard_map(body, mesh=mesh, in_specs=in_specs, out_specs=out_specs, check_vma=False)
```

time: 1580 us -> 107 us (0.07)
  waiting for transfers between devices: 1310 us -> 0 us
  other arithmetic: 141 us -> 0 us
  Pallas kernels: 0 us -> 102 us
  starting transfers between devices: 47.1 us -> 0 us
  blocking collectives: 32.6 us -> 0 us
  matrix products: 21.1 us -> 0 us
    unnamed x4 -> x0, waiting for transfers between devices: 682 us -> none
    psum x1 -> x0, waiting for transfers between devices: 481 us -> none  [body(): summed = lax.psum(contract_rows(embeddings, sketched), ('grp', 'dev'))]
    all_gather x1 -> x0, waiting for transfers between devices: 138 us -> none  [body(): lax.all_gather(sketch_matrix, 'dev', axis=0, tiled=True)]
    another operation x32 -> x0, other arithmetic: 135 us -> none  [the longest x27 111 us: merge_factor(): return jnp.linalg.cholesky(summed)]
    pallas_call x0 -> x1, Pallas kernels: none -> 102 us  [body(): pl.pallas_call(kernel, out_shape=(jax.ShapeDtypeStruct((rows, k), F32), j...]
    ppermute x9 -> x0, starting transfers between devices: 47 us -> none  [swapped(): lax.ppermute(x, axis, [(i, i ^ 1 << apart) for i in range(lax.axis_size(a...]
    psum x1 -> x0, blocking collectives: 32.6 us -> none  [body(): projected = lax.psum(partial_rows, 'grp') * out_scale]
    dot_general x22 -> x0, matrix products: 19.8 us -> none  [the longest x9 8.22 us: merge_factor(): jnp.dot(triangle, triangle.T, precision=lax.Precision.HIGHEST)]
  transfers between devices with their start and end apart: 12 -> 0, of which waited for: 11 -> 0; matrix products, arithmetic and copies ran while one was open for 1% -> 0% of each run, Pallas kernels for 0% -> 0%
where the time goes in v1:
time: 107 us
  Pallas kernels  102 us (95%)
  local copies, waits for them, and re-layouts  3.89 us (4%)
    pallas_call x1, Pallas kernels, body(): pl.pallas_call(kernel, out_shape=(jax.ShapeDtypeStruct((rows, k), F32), j...  102 us
    unnamed x6, local copies, waits for them, and re-layouts  3.89 us

profile of v1, /device:TPU:1, one launch (start us, length us, event | category | flops | bytes accessed | tf_op | source)
XLA Modules:
  0.0 106.5 jit_solution(8520690854649405667)
XLA Ops:
  0.6 0.0 copy-start
  0.6 1.9 %copy-done = bf16[384,4096]{1,0:T(8,128)(2,1)S(1)} copy-done((bf16[384,4096]{1,0:T(8,128)(2,1)S(1)}, bf16[384,4096]{1,0:T(8,128)(2,1)}, u32[]{:S(2)}) %copy-start) | copy-done | bytes 3145752
  2.5 0.0 copy-start.1
  2.5 0.7 copy-done.1
  3.2 102.0 %shard_map.41 = (f32[384,128]{1,0:T(8,128)S(1)}, f32[64,128]{1,0:T(8,128)S(1)}) custom-call(bf16[384,4096]{1,0:T(8,128)(2,1)S(1)} %copy-done, bf16[64,128]{1,0:T(8,128)(2,1)S(1)} %copy-done.1), custom_call_target="tpu_custom_call" | custom-call | flops 1610612736 | bytes 3145728 | tf_op jit(solution)/shard_map/pallas_call | solution.py:341
  105.2 0.7 copy.6
  105.9 0.6 copy.7
Async XLA Ops:
  0.6 1.9 %copy-start = (bf16[384,4096]{1,0:T(8,128)(2,1)S(1)}, bf16[384,4096]{1,0:T(8,128)(2,1)}, u32[]{:S(2)}) copy-start(bf16[384,4096]{1,0:T(8,128)(2,1)} %e_hbm.1) | copy-start | bytes 9437188
  2.5 0.7 copy-start.1

commit v2 on v1

v2 whole, which is shorter than its diff:
```python
import jax
import jax.numpy as jnp
from jax import lax
from jax.experimental import pallas as pl
from jax.experimental.pallas import tpu as pltpu
from jax.sharding import PartitionSpec as P

X, Y, Z, C = 4, 4, 16, 2
XY = X * Y
ZL = Z // C
DEVICES = XY * Z * C
PIECE = 16
CHUNK = ZL * Y * PIECE
PANEL = 16
BLOCKS = 2
HIGHEST = lax.Precision.HIGHEST
F32, BF16 = jnp.float32, jnp.bfloat16


def far_first(steps, *sizes):
    def hops(k):
        total = 0
        for size in reversed(sizes):
            total += min(k % size, size - k % size)
            k //= size
        return total

    return sorted(steps, key=lambda k: -hops(k))


PLANE = far_first(range(1, XY), X, Y)
LINE = far_first(range(1, Z), Z)
RING = far_first(range(X), X)


def nt(a, b, precision=None):
    return lax.dot_general(
        a, b, (((1,), (1,)), ((), ())), precision=precision, preferred_element_type=F32
    )


def tn(a, b, precision=None):
    return lax.dot_general(
        a, b, (((0,), (0,)), ((), ())), precision=precision, preferred_element_type=F32
    )


def nn(a, b, precision=None):
    return jnp.dot(a, b, precision=precision, preferred_element_type=F32)


def inverse_factor(gram):
    k = gram.shape[0]
    rows = lax.broadcasted_iota(jnp.int32, (PANEL, 1), 0)
    eye = (
        lax.broadcasted_iota(jnp.int32, (k, k), 0) == lax.broadcasted_iota(jnp.int32, (k, k), 1)
    ).astype(F32)
    trailing = jnp.concatenate([gram, eye], axis=1)
    done = []
    for base in range(0, k, PANEL):
        panel = trailing[:PANEL]
        cols = [
            jnp.broadcast_to(panel[:, base + t : base + t + 1], (PANEL, k)) for t in range(PANEL)
        ]
        left, right = panel[:, :k], panel[:, k:]
        for j in range(PANEL):
            pivot = lax.rsqrt(cols[j][j : j + 1])
            factor = cols[j] * pivot
            below = jnp.where(rows > j, factor, 0.0)
            for t in range(j + 1, PANEL):
                cols[t] = cols[t] - below * factor[t : t + 1]
            scale = jnp.where(rows == j, pivot, 1.0)
            left_row, right_row = left[j : j + 1] * pivot, right[j : j + 1] * pivot
            left = left * scale - below * left_row
            right = right * scale - below * right_row
        done.append(right)
        if base + PANEL < k:
            both = jnp.concatenate([left, right], axis=1)
            trailing = trailing[PANEL:] - tn(left[:, base + PANEL :], both, HIGHEST)
    return jnp.concatenate(done, axis=0)


def kernel(
    e_hbm, s_hbm, ortho_ref, proj_ref,
    e_chip, s_piece, s_half, p_half, mine_a, mine_b, theirs_a, theirs_b, right_a, right_b, refined,
    sum_a, sum_b, xy_a, xy_b, zout_a, zout_b, z_a, z_b, gpart, g1, g2, gfull, y_all,
    load_sem, piece_sem, e_s, e_r,
    ags_z_s, ags_z_r, ags_x_s, ags_x_r, ags_c_s, ags_c_r,
    agp_z_s, agp_z_r, agp_x_s, agp_x_r, agp_c_s, agp_c_r,
    rsa_x_s, rsa_x_r, rsa_z_s, rsa_z_r,
    rsb_x_s, rsb_x_r, rsb_z_s, rsb_z_r,
    g1_s, g1_r, g2_s, g2_r, g3_s, g3_r, f_s, f_r,
):
    grp, dev = lax.axis_index("grp"), lax.axis_index("dev")
    y, c = grp // C, grp % C
    x, z = dev // Z, dev % Z
    other = 1 - c
    half, zl = z // ZL, z % ZL
    owner = c == half
    rows, width = e_hbm.shape
    k_all = s_hbm.shape[1]
    rows_all = DEVICES * rows

    def at(x_, y_, z_, c_):
        return (y_ * C + c_, x_ * Z + z_)

    def xy(k):
        kx, ky = k // Y, k % Y
        return ((x + kx) % X, (y + ky) % Y), ((x + X - kx) % X, (y + Y - ky) % Y)

    drains, earlier = [], []

    def drain_earlier():
        for drain in earlier:
            drain()
        earlier[:] = drains
        drains.clear()

    def send(src, dst, ssem, rsem, to, when=None):
        copy = pltpu.make_async_remote_copy(
            src_ref=src, dst_ref=dst, send_sem=ssem, recv_sem=rsem,
            device_id=to, device_id_type=pl.DeviceIdType.MESH,
        )

        def start():
            copy.start()

        def drain():
            copy.wait_send()

        if when is None:
            start()
            drains.append(drain)
        else:
            pl.when(when)(start)
            drains.append(lambda: pl.when(when)(drain))

    def receive(dst, ssem, rsem, when=None):
        copy = pltpu.make_async_remote_copy(
            src_ref=dst, dst_ref=dst, send_sem=ssem, recv_sem=rsem,
            device_id=at(x, y, z, other), device_id_type=pl.DeviceIdType.MESH,
        )
        if when is None:
            copy.wait_recv()
        else:
            pl.when(when)(copy.wait_recv)

    def columns(x_, half_):
        return e_hbm.at[:, pl.ds(pl.multiple_of((x_ * C + half_) * CHUNK, CHUNK), CHUNK)]

    def load(x_):
        return pltpu.make_async_copy(columns(x_, c), e_chip.at[x_, pl.ds(0, rows)], load_sem.at[x_])

    for x_ in range(X):
        load(x_).start()
    load_piece = pltpu.make_async_copy(
        s_hbm.at[pl.ds(pl.multiple_of(y * PIECE, PIECE), PIECE)], s_piece, piece_sem
    )
    load_piece.start()

    barrier = pltpu.get_barrier_semaphore()

    def greet(to):
        pl.semaphore_signal(barrier, inc=1, device_id=to, device_id_type=pl.DeviceIdType.MESH)

    for k in LINE:
        greet(at(x, y, (z + k) % Z, c))
    for k in PLANE:
        (x_, y_), _b = xy(k)
        for c_ in range(C):
            greet(at(x_, y_, z, c_))
    greet(at(x, y, z, other))

    load_piece.wait()
    for x_ in range(X):
        load(x_).wait()
    pl.semaphore_wait(barrier, XY * C - 1 + Z - 1)

    def exchange_embeddings():
        for x_ in range(X):
            send(
                columns(x_, other), e_chip.at[x_, pl.ds(rows, rows)],
                e_s.at[x_], e_r.at[x_], at(x, y, z, other),
            )
        for x_ in range(X):
            receive(e_chip.at[x_, pl.ds(rows, rows)], e_s.at[x_], e_r.at[x_])

    def gather_times(piece, meanwhile, use, full, mine_ref, theirs, z_s, z_r, x_s, x_r, c_s, c_r):
        @pl.when(owner)
        def _():
            full[x, y, zl] = piece()

        for k in LINE:
            mine = full.at[x, y, zl]
            send(mine, mine, z_s.at[k], z_r.at[zl], at(x, y, (z + k) % Z, c), owner)
        drain_earlier()
        meanwhile()
        for k in range(ZL):
            low = (zl + k) % ZL
            receive(
                full.at[x, y, low], z_s.at[0], z_r.at[low],
                jnp.logical_not(owner) if k == 0 else None,
            )
        mine = full.at[x, y]
        for k in PLANE:
            (x_, y_), _b = xy(k)
            send(mine, mine, x_s.at[k], x_r.at[k], at(x_, y_, z, c))
        drain_earlier()

        depth = C * rows // BLOCKS
        for kx in reversed(RING):
            for ky in reversed(RING):
                k = kx * Y + ky
                if k:
                    _f, (x_, y_) = xy(k)
                    receive(full.at[x_, y_], x_s.at[k], x_r.at[k])
            x_ = (x + X - kx) % X
            block = full[x_]
            block = jnp.concatenate(
                [block[y_, low] for low in range(ZL) for y_ in range(Y)], axis=0
            )
            for b in range(BLOCKS):
                here = pl.ds(b * depth, depth)
                term = nn(e_chip[x_, here], block)
                mine_ref[here] = term if kx == 0 else mine_ref[here] + term
                if kx == RING[0]:
                    send(
                        mine_ref.at[here], theirs.at[here], c_s.at[b], c_r.at[b],
                        at(x, y, z, other),
                    )
        for b in range(BLOCKS):
            there = pl.ds(b * depth, depth)
            here = pl.ds((b + BLOCKS // C) % BLOCKS * depth, depth)
            receive(theirs.at[there], c_s.at[b], c_r.at[b])
            use(here, mine_ref[here] + theirs[there])

    def scatter_first(right, summed, landing, x_s, x_r):
        for kx in RING:
            block = tn(e_chip[(x + kx) % X], right[...]).astype(BF16)
            block = block.reshape(ZL, Y, PIECE, right.shape[1])
            for y_ in range(Y):
                summed[kx, y_] = block[:, y_]
            for ky in RING:
                k = kx * Y + ky
                if k:
                    (x_, y_), _b = xy(k)
                    send(
                        summed.at[kx, y_], landing.at[k], x_s.at[k], x_r.at[k], at(x_, y_, z, c)
                    )
        drain_earlier()

    def scatter_second(summed, landing, x_s, x_r, zout, zland, z_s, z_r):
        total = summed[0, y].astype(F32)
        for k in reversed(PLANE):
            receive(landing.at[k], x_s.at[k], x_r.at[k])
            total = total + landing[k].astype(F32)
        zout[...] = total.astype(BF16)
        apart = (c - half) * (c - half)
        for i in range(ZL):
            near, far = ((j + 1) // 2 * (1 if j % 2 else ZL - 1) % ZL for j in (ZL - 1 - i, i))
            low = (zl + near + apart * (far - near + ZL)) % ZL
            send(
                zout.at[low], zland.at[z], z_s.at[i], z_r.at[z], at(x, y, c * ZL + low, c),
                jnp.logical_not(owner) if i == ZL - 1 else None,
            )
        drain_earlier()

    def scatter_third(zout, zland, z_s, z_r):
        zland[z] = zout[zl]
        total = None
        for k in reversed(LINE):
            from_ = (z + k) % Z
            receive(zland.at[from_], z_s.at[0], z_r.at[from_])
        for k in range(Z):
            term = zland[k].astype(F32)
            total = term if total is None else total + term
        return total

    def keep_sketched(here, block):
        right_a[here] = block.astype(BF16)

    gather_times(
        lambda: s_piece[...], exchange_embeddings, keep_sketched,
        s_half, mine_a, theirs_a, ags_z_s, ags_z_r, ags_x_s, ags_x_r, ags_c_s, ags_c_r,
    )

    scatter_first(right_a, sum_a, xy_a, rsa_x_s, rsa_x_r)
    scatter_second(sum_a, xy_a, rsa_x_s, rsa_x_r, zout_a, z_a, rsa_z_s, rsa_z_r)

    def keep_refined(here, block):
        right_b[here] = block.astype(BF16)
        refined[here] = block

    gather_times(
        lambda: (scatter_third(zout_a, z_a, rsa_z_s, rsa_z_r) / rows_all).astype(BF16),
        lambda: None, keep_refined,
        p_half, mine_b, theirs_b, agp_z_s, agp_z_r, agp_x_s, agp_x_r, agp_c_s, agp_c_r,
    )

    gram = tn(refined[...], refined[...], HIGHEST) / rows_all
    gpart[...] = gram.reshape(gpart.shape)

    keeper = c == (x + y) % C
    for k in PLANE:
        (x_, y_), _b = xy(k)
        odd = (k // Y + k % Y) % C
        send(
            gpart.at[x_ * Y + y_], g1.at[k], g1_s.at[k], g1_r.at[k],
            at(x_, y_, z, c), jnp.logical_not(keeper) if odd else keeper,
        )

    scatter_first(right_b, sum_b, xy_b, rsb_x_s, rsb_x_r)

    @pl.when(keeper)
    def _():
        g1[0] = gpart[x * Y + y]
        for k in reversed(PLANE):
            receive(g1.at[k], g1_s.at[0], g1_r.at[k])
        g2[z] = jnp.sum(g1[...], axis=0)

    for k in LINE:
        send(g2.at[z], g2.at[z], g2_s.at[k], g2_r.at[z], at(x, y, (z + k) % Z, c), keeper)

    scatter_second(sum_b, xy_b, rsb_x_s, rsb_x_r, zout_b, z_b, rsb_z_s, rsb_z_r)

    @pl.when(keeper)
    def _():
        for k in reversed(LINE):
            from_ = (z + k) % Z
            receive(g2.at[from_], g2_s.at[0], g2_r.at[from_])
        gfull[x * Y + y] = jnp.sum(g2[...], axis=0)

    mine = gfull.at[x * Y + y]
    for k in (*PLANE, 0):
        (x_, y_), _b = xy(k)
        for c_ in (other, c) if k else (other,):
            i = C * k + (c_ is c)
            send(mine, mine, g3_s.at[i], g3_r.at[k], at(x_, y_, z, c_), keeper)

    @pl.when(owner)
    def _():
        y_all[y] = scatter_third(zout_b, z_b, rsb_z_s, rsb_z_r)

    for j in far_first(range(1, Y * C), Y, C):
        y_, c_ = (y + j // C) % Y, (c + j % C) % C
        send(y_all.at[y], y_all.at[y], f_s.at[j], f_r.at[y], at(x, y_, z, c_), owner)
    drain_earlier()
    drain_earlier()
    for k in (0, *reversed(PLANE)):
        _f, (x_, y_) = xy(k)
        receive(
            gfull.at[x_ * Y + y_], g3_s.at[0], g3_r.at[k], None if k else jnp.logical_not(keeper)
        )

    inverse = inverse_factor(gfull[...].reshape(k_all, k_all))

    ortho_ref[...] = nt(refined[pl.ds(0, rows)], inverse, HIGHEST)
    for k in (0, 3, 1, 2):
        from_ = (y + k) % Y
        receive(
            y_all.at[from_], f_s.at[0], f_r.at[from_], None if k else jnp.logical_not(owner)
        )
    proj_ref[...] = nt(y_all[...].reshape(proj_ref.shape), inverse, HIGHEST) * (
        width**0.5 / rows_all
    )

    drain_earlier()
    drain_earlier()


def body(embeddings, sketch_matrix):
    rows, width = embeddings.shape
    k = sketch_matrix.shape[1]
    dma = pltpu.SemaphoreType.DMA
    half = pltpu.VMEM((X, Y, ZL, PIECE, k), BF16)
    partial = pltpu.VMEM((C * rows, k), F32)
    right = pltpu.VMEM((C * rows, k), BF16)
    landing = pltpu.VMEM((XY, ZL, PIECE, k), BF16)
    zout = pltpu.VMEM((ZL, PIECE, k), BF16)
    zland = pltpu.VMEM((Z, PIECE, k), BF16)
    gather_sems = [dma((Z,)), dma((ZL,)), dma((XY,)), dma((XY,))]
    gather_sems += [dma((BLOCKS,)), dma((BLOCKS,))]
    scatter_sems = [dma((XY,)), dma((XY,)), dma((ZL,)), dma((Z,))]
    return pl.pallas_call(
        kernel,
        out_shape=(
            jax.ShapeDtypeStruct((rows, k), F32),
            jax.ShapeDtypeStruct(sketch_matrix.shape, F32),
        ),
        in_specs=[pl.BlockSpec(memory_space=pltpu.HBM)] * 2,
        out_specs=[pl.BlockSpec(memory_space=pltpu.VMEM)] * 2,
        scratch_shapes=[
            pltpu.VMEM((X, C * rows, CHUNK), BF16),
            pltpu.VMEM((PIECE, k), BF16),
            half, half, partial, partial, partial, partial, right, right, partial, half, half, landing, landing,
            zout, zout, zland, zland,
            pltpu.VMEM((XY, k // XY, k), F32),
            pltpu.VMEM((XY, k // XY, k), F32),
            pltpu.VMEM((Z, k // XY, k), F32),
            pltpu.VMEM((XY, k // XY, k), F32),
            pltpu.VMEM((Y, PIECE, k), F32),
            dma((X,)), dma, dma((X,)), dma((X,)),
            *gather_sems, *gather_sems, *scatter_sems, *scatter_sems,
            dma((XY,)), dma((XY,)), dma((Z,)), dma((Z,)), dma((XY * C,)), dma((XY,)),
            dma((Y * C,)), dma((Y,)),
        ],
        compiler_params=pltpu.CompilerParams(
            collective_id=0, has_side_effects=True, vmem_limit_bytes=52 * 1024 * 1024
        ),
        cost_estimate=pl.CostEstimate(
            flops=8 * rows * width * k, bytes_accessed=2 * rows * width, transcendentals=0
        ),
    )(embeddings, sketch_matrix)


def solution(mesh):
    in_specs = (P(("grp", "dev"), None), P("dev", None))
    out_specs = (P(("grp", "dev"), None), P("dev", None))
    return jax.shard_map(body, mesh=mesh, in_specs=in_specs, out_specs=out_specs, check_vma=False)
```

time: 107 us -> 94.1 us (0.88); the launches traced: 107 us -> 92.3 us
  Pallas kernels: 102 us -> 89.7 us
  local copies, waits for them, and re-layouts: 3.89 us -> 2 us
    pallas_call x1, Pallas kernels: 102 us -> 89.7 us  [body(): pl.pallas_call(kernel, out_shape=(jax.ShapeDtypeStruct((rows, k), F32), j...]
    unnamed x6 -> x4, local copies, waits for them, and re-layouts: 3.89 us -> 2 us
where the time goes in v2:
time: 94.1 us; the launch traced here: 92.3 us
  Pallas kernels  89.7 us (95%)
  local copies, waits for them, and re-layouts  2 us (2%)
    pallas_call x1, Pallas kernels, body(): pl.pallas_call(kernel, out_shape=(jax.ShapeDtypeStruct((rows, k), F32), j...  89.7 us
    unnamed x4, local copies, waits for them, and re-layouts  2 us

profile of v2, /device:TPU:1, one launch (start us, length us, event | category | flops | bytes accessed | tf_op | source)
XLA Modules:
  0.0 92.3 jit_solution(1300486414167069817)
XLA Ops:
  0.6 0.0 copy-start
  0.6 0.7 copy-done
  1.3 89.7 %shard_map.41 = (f32[384,128]{1,0:T(8,128)S(1)}, f32[64,128]{1,0:T(8,128)S(1)}) custom-call(bf16[384,4096]{1,0:T(8,128)(2,1)} %e_hbm.1, bf16[64,128]{1,0:T(8,128)(2,1)S(1)} %copy-done), custom_call_target="tpu_custom_call" | custom-call | flops 1610612736 | bytes 3145728 | tf_op jit(solution)/shard_map/pallas_call | solution.py:384
  91.0 0.7 copy.6
  91.7 0.6 copy.7
Async XLA Ops:
  0.6 0.7 copy-start

commit v3 on v2

--- a/solution.py
+++ b/solution.py
@@ -11,7 +11,7 @@
 DEVICES = XY * Z * C
 PIECE = 16
 CHUNK = ZL * Y * PIECE
-PANEL = 16
+PANEL = 32
 BLOCKS = 2
 HIGHEST = lax.Precision.HIGHEST
 F32, BF16 = jnp.float32, jnp.bfloat16

time: 94.1 us -> 93.7 us (level)
  no operation moved by 1% of the time
where the time goes in v3:
time: 93.7 us; the launch traced here: 92.1 us
  Pallas kernels  89.5 us (96%)
  local copies, waits for them, and re-layouts  2 us (2%)
    pallas_call x1, Pallas kernels, body(): pl.pallas_call(kernel, out_shape=(jax.ShapeDtypeStruct((rows, k), F32), j...  89.5 us
    unnamed x4, local copies, waits for them, and re-layouts  2 us

profile of v3, /device:TPU:1, one launch (start us, length us, event | category | flops | bytes accessed | tf_op | source)
XLA Modules:
  0.0 92.1 jit_solution(2971564703254161938)
XLA Ops:
  0.6 0.0 copy-start
  0.6 0.7 copy-done
  1.3 89.5 %shard_map.41 = (f32[384,128]{1,0:T(8,128)S(1)}, f32[64,128]{1,0:T(8,128)S(1)}) custom-call(bf16[384,4096]{1,0:T(8,128)(2,1)} %e_hbm.1, bf16[64,128]{1,0:T(8,128)(2,1)S(1)} %copy-done), custom_call_target="tpu_custom_call" | custom-call | flops 1610612736 | bytes 3145728 | tf_op jit(solution)/shard_map/pallas_call | solution.py:384
  90.8 0.7 copy.6
  91.5 0.6 copy.7
Async XLA Ops:
  0.6 0.7 copy-start
